TPU v7x, 32 devices: a whole 2x2x4 slice. The times are simulated.
32 devices in a mesh: gx: 4 (over x, core), gy: 2 (over y), gz: 4 (over z).
Axes of the slice: x: 2, y: 2, z: 4, core: 2. Of those that a mesh axis runs over, the one named last changes fastest.
Arguments:
- positions: float32 [3, 4, 2, 8, 256], P(None, 'gx', 'gy', 'gz'), may hold values from 0 to 1
- velocities: float32 [3, 4, 2, 8, 256], P(None, 'gx', 'gy', 'gz'), may hold values from -2 to 2
- mass: float32 [4, 2, 8, 256], P('gx', 'gy', 'gz'), may hold values from 0.03 to 0.3
- counts: int32 [4, 2, 8], P('gx', 'gy', 'gz'), may hold values from 1 to 256, as said below
Outputs:
- new_positions: float32 [3, 4, 2, 8, 256], P(None, 'gx', 'gy', 'gz')
- new_velocities: float32 [3, 4, 2, 8, 256], P(None, 'gx', 'gy', 'gz')
Inputs may be any that keep to these rules, and one draw needn't show every extreme that they name: `counts`: particles of a bin fill its first slots; every bin holds at least 128 particles, and some bin holds exactly 256 particles in every draw.
All inputs are finite; a program needn't handle non-finite values.
Results may differ from a plain program's by a relative error of at most 0.0001.
Values sent between devices are 32-bit elements; how exact they have to be, the bound alone decides.
No kernel may reach another device: no remote copies, remote signals or barrier semaphores. Data moves between devices by JAX's collectives and lax.ppermute only.
A program may use at most 64 MiB of HBM per device.

v0:
```python
import functools

import jax
import jax.numpy as jnp
from jax import lax
from jax.experimental import pallas as pl
from jax.experimental.pallas import tpu as pltpu
from jax.sharding import PartitionSpec as P

SUBCYCLES = 2

time_step = 0.25

CENTRE = (0.5, 0.5, 1.0)
F32, BF16 = jnp.float32, jnp.bfloat16


def parts(value):
    high = value.astype(BF16).astype(F32)
    rest = value - high
    mid = rest.astype(BF16).astype(F32)
    return high, mid, rest - mid


def row_index(rows, slots):
    return lax.broadcasted_iota(jnp.int32, (rows, slots), 0)


def shifted(packed, offset):
    row = row_index(*packed.shape)
    move = jnp.where(row == 0, offset[0], jnp.where(row == 1, offset[1], jnp.where(row == 2, offset[2], 0.0)))
    return packed + move.astype(F32)


def source_rows(packed, offset):
    slots = packed.shape[-1]
    moved = shifted(packed, offset)
    row = row_index(4, slots)
    square = jnp.sum(jnp.where(row < 3, moved * moved, 0.0), axis=0, keepdims=True)
    head = jnp.where(row < 3, moved, square)
    tail = jnp.where(row == 0, 1.0, 0.0).astype(F32)
    high, mid, low = parts(jnp.concatenate([head, tail], axis=0))
    distance = jnp.concatenate([high, high, high, mid, mid, low], axis=0).astype(BF16)
    mass = moved[3:4]
    carried = jnp.where(row < 3, moved * mass, mass)
    high, mid, low = parts(jnp.concatenate([carried, jnp.zeros_like(carried)], axis=0))
    summed = jnp.concatenate([high, mid, low, jnp.zeros_like(low)], axis=0).astype(BF16)
    return distance, summed


def target_rows(moved):
    slots = moved.shape[-1]
    row = row_index(4, slots)
    square = jnp.sum(jnp.where(row < 3, moved * moved, 0.0), axis=0, keepdims=True)
    head = jnp.where(row < 3, 2.0 * moved, -1.0)
    tail = jnp.where(row == 0, 1.0 - square, 0.0)
    high, mid, low = parts(jnp.concatenate([head, tail], axis=0))
    return jnp.concatenate([high, mid, low, high, mid, high], axis=0).T.astype(BF16)


def pair_weight(target, source):
    near = jnp.maximum(jnp.dot(target, source, preferred_element_type=F32), 0.0)
    weight = near * near * near
    high = weight.astype(BF16)
    return high, (weight - high.astype(F32)).astype(BF16)


def contract(weights, rows):
    return lax.dot_general(rows, weights, (((1,), (1,)), ((), ())), preferred_element_type=F32)


def occupied(counts_ref, z, shape):
    return lax.broadcasted_iota(jnp.int32, shape, 1) < counts_ref[0, 0, z]


def pack_kernel(counts_ref, place_ref, mass_ref, packed_ref):
    for z in range(2):
        mass = mass_ref[0, 0, z : z + 1, :]
        weight = jnp.where(occupied(counts_ref, z, mass.shape), mass, 0.0)
        rows = [place_ref[c, 0, 0, z : z + 1, :] for c in range(3)]
        packed_ref[z] = jnp.concatenate(rows + [weight], axis=0)


def gather_column(size_x, size_y):
    here_x, here_y = lax.axis_index("gx"), lax.axis_index("gy")
    places = []
    for x in (-1, 0, 1):
        for y in (-1, 0, 1):
            place = lax.rem(here_x + (x + size_x), size_x) * size_y + lax.rem(here_y + (y + size_y), size_y)
            places.append((place, x - CENTRE[0], y - CENTRE[1]))
    return places


def fill(refs, levels, sizes, near_ref, sum_ref):
    for column, (place, x, y) in enumerate(gather_column(*sizes)):
        for slot, (ref, level) in enumerate(zip(refs, levels)):
            distance, summed = source_rows(ref[place], (x, y, level - CENTRE[2]))
            near_ref[column, slot] = distance
            sum_ref[column, slot] = summed


def target_places(own_ref):
    own = [own_ref[z] for z in range(2)]
    return own, [shifted(own[z], (-CENTRE[0], -CENTRE[1], z - CENTRE[2])) for z in range(2)]


def totals_over(targets, wanted, near_ref, sum_ref, totals):
    def column_step(column, totals):
        out = []
        for z in range(2):
            total = totals[z]
            for slot in wanted[z]:
                high, low = pair_weight(targets[z], near_ref[column, slot])
                rows = sum_ref[column, slot]
                total = total + contract(high, rows) + contract(low, rows)
            out.append(total)
        return tuple(out)

    return lax.fori_loop(0, near_ref.shape[0], column_step, tuple(totals))


def inner_kernel(sizes, own_ref, low_ref, high_ref, total_ref, near_ref, sum_ref):
    _, moved = target_places(own_ref)
    targets = [target_rows(m) for m in moved]
    fill((low_ref, high_ref), (0, 1), sizes, near_ref, sum_ref)
    zero = jnp.zeros(total_ref.shape[1:], F32)
    totals = totals_over(targets, ((0, 1), (0, 1)), near_ref, sum_ref, (zero, zero))
    for z in range(2):
        total_ref[z] = totals[z]


def outer_kernel(sizes, first, last, counts_ref, speed_ref, own_ref, total_ref, below_ref, above_ref, *refs):
    if last:
        place_out, speed_out, near_ref, sum_ref = refs
    else:
        packed_out, speed_out, near_ref, sum_ref = refs
    own, moved = target_places(own_ref)
    targets = [target_rows(m) for m in moved]
    fill((below_ref, above_ref), (-1, 2), sizes, near_ref, sum_ref)
    totals = totals_over(targets, ((0,), (1,)), near_ref, sum_ref, (total_ref[0], total_ref[1]))
    slots = own[0].shape[-1]
    for z in range(2):
        total = totals[z][0:8] + totals[z][8:16] + totals[z][16:24]
        total = total[0:4]
        accel = total - moved[z] * total[3:4]
        if first:
            speed = jnp.concatenate([speed_ref[c, 0, 0, z : z + 1, :] for c in range(3)] + [jnp.zeros((1, slots), F32)], axis=0)
        else:
            speed = speed_ref[z]
        speed = speed + time_step * accel
        place = jnp.clip(own[z] + time_step * speed, 0.0, 1.0)
        if last:
            keep = occupied(counts_ref, z, (1, slots))
            for c in range(3):
                place_out[c, 0, 0, z : z + 1, :] = jnp.where(keep, place[c : c + 1], 0.0)
                speed_out[c, 0, 0, z : z + 1, :] = jnp.where(keep, speed[c : c + 1], 0.0)
        else:
            row = row_index(4, slots)
            packed_out[z] = jnp.where(row < 3, place, own[z])
            speed_out[z] = speed


VMEM = pl.BlockSpec(memory_space=pltpu.VMEM)
SMEM = pl.BlockSpec(memory_space=pltpu.SMEM)
PARAMS = pltpu.CompilerParams(vmem_limit_bytes=32 * 1024 * 1024)


def ring(axis, step):
    size = lax.axis_size(axis)
    return [(i, (i + step) % size) for i in range(size)]


def cost(pairs, slots):
    return pl.CostEstimate(flops=pairs * slots * slots * 200, bytes_accessed=1 << 18, transcendentals=0)


def on_device(positions, velocities, mass, counts):
    slots = positions.shape[-1]
    sizes = (lax.axis_size("gx"), lax.axis_size("gy"))
    columns = sizes[0] * sizes[1]
    bins = jax.ShapeDtypeStruct((2, 4, slots), F32)
    full = jax.ShapeDtypeStruct(positions.shape, F32)
    packed = pl.pallas_call(
        pack_kernel,
        out_shape=bins,
        in_specs=[SMEM, VMEM, VMEM],
        out_specs=VMEM,
    )(counts, positions, mass)
    speed = velocities
    for subcycle in range(SUBCYCLES):
        first, last = subcycle == 0, subcycle == SUBCYCLES - 1
        copies = jnp.broadcast_to(packed[:, None], (2, columns, 4, slots))
        planes = lax.all_to_all(copies, ("gx", "gy"), 1, 1, tiled=True)
        low, high = planes[0], planes[1]
        below = lax.ppermute(high, "gz", ring("gz", 1))
        above = lax.ppermute(low, "gz", ring("gz", -1))
        total = pl.pallas_call(
            functools.partial(inner_kernel, sizes),
            out_shape=jax.ShapeDtypeStruct((2, 32, slots), F32),
            in_specs=[VMEM] * 3,
            out_specs=VMEM,
            scratch_shapes=[pltpu.VMEM((9, 2, 48, slots), BF16), pltpu.VMEM((9, 2, 32, slots), BF16)],
            compiler_params=PARAMS,
            cost_estimate=cost(36, slots),
        )(packed, low, high)
        packed, speed = pl.pallas_call(
            functools.partial(outer_kernel, sizes, first, last),
            out_shape=(full, full) if last else (bins, bins),
            in_specs=[SMEM] + [VMEM] * 5,
            out_specs=(VMEM, VMEM),
            scratch_shapes=[pltpu.VMEM((9, 2, 48, slots), BF16), pltpu.VMEM((9, 2, 32, slots), BF16)],
            compiler_params=PARAMS,
            cost_estimate=cost(18, slots),
        )(counts, speed, packed, total, below, above)
    return packed, speed


def solution(mesh):
    placed = (
        P(None, "gx", "gy", "gz", None),
        P(None, "gx", "gy", "gz", None),
        P("gx", "gy", "gz", None),
        P("gx", "gy", "gz"),
    )
    return jax.shard_map(
        on_device,
        mesh=mesh,
        in_specs=placed,
        out_specs=(P(None, "gx", "gy", "gz", None), P(None, "gx", "gy", "gz", None)),
        check_vma=False,
    )
```

profile of v0, /device:TPU:0, one launch (start us, length us, event | category | flops | bytes accessed | tf_op | source)
XLA Modules:
  0.0 51.9 jit_solution(4121884546169078392)
XLA Ops:
  0.6 1.3 %shard_map.59.own_ref = f32[2,4,256]{2,1,0:T(4,128)} custom-call(s32[1,1,2]{2,1,0:T(1,128)} %counts_ref.5, f32[3,1,1,2,256]{4,3,2,1,0:T(2,128)} %place_ref.1, f32[1,1,2,256]{3,2,1,0:T(2,128)} %mass_ref.1), custom_call_target="tpu_custom_call" | custom-call | tf_op jit(solution)/shard_map/pallas_call | solution.py:183
  1.9 0.7 %broadcast_in_dim.4 = f32[2,8,4,256]{3,2,0,1:T(4,128)S(1)} broadcast(f32[2,4,256]{2,1,0:T(4,128)} %shard_map.59.own_ref), dimensions={0,2,3} | broadcast | bytes 73728 | tf_op jit(solution)/shard_map/broadcast_in_dim | solution.py:192
  2.7 9.7 %all_to_all.10 = f32[2,8,4,256]{3,2,0,1:T(4,128)S(1)} all-to-all(f32[2,8,4,256]{3,2,0,1:T(4,128)S(1)} %broadcast_in_dim.4), channel_id=1, replica_groups=mesh['gx'=4,'gy'=2,'gz'=4] {'gx','gy'}, dimensions={1} | all-to-all | bytes 131072 | tf_op jit(solution)/shard_map/all_to_all | solution.py:193
  12.4 0.0 copy-start
  12.4 1.6 %collective-permute-start = (f32[8,4,256]{2,1,0:T(4,128)S(1)}, f32[8,4,256]{2,1,0:T(4,128)S(1)}, u32[]{:S(2)}, u32[]{:S(2)}) collective-permute-start(f32[8,4,256]{2,1,0:T(4,128)S(1)} %get-tuple-element.8.high_ref), channel_id=1, source_target_pairs={{0,1},{1,2},{2,3},{3,0},{4,5},{5,6},{6,7},{7,4},{8,9},{9,10},{10,1... | collective-permute-start | bytes 98312 | tf_op jit(solution)/shard_map/ppermute | solution.py:195
  14.0 0.0 copy-start.1
  14.0 0.0 copy-start.2
  14.0 2.2 %collective-permute-start.1 = (f32[8,4,256]{2,1,0:T(4,128)S(1)}, f32[8,4,256]{2,1,0:T(4,128)S(1)}, u32[]{:S(2)}, u32[]{:S(2)}) collective-permute-start(f32[8,4,256]{2,1,0:T(4,128)S(1)} %get-tuple-element.9.low_ref), channel_id=1, source_target_pairs={{0,3},{1,0},{2,1},{3,2},{4,7},{5,4},{6,5},{7,6},{8,11},{9,8},{10,9... | collective-permute-start | bytes 98312 | tf_op jit(solution)/shard_map/ppermute | solution.py:196
  16.3 0.0 copy-done
  16.3 7.4 %shard_map.60.total_ref = f32[2,32,256]{2,1,0:T(8,128)S(1)} custom-call(f32[2,4,256]{2,1,0:T(4,128)S(1)} %copy-done, f32[8,4,256]{2,1,0:T(4,128)S(1)} %get-tuple-element.9.low_ref, f32[8,4,256]{2,1,0:T(4,128)S(1)} %get-tuple-element.8.high_ref), custom_call_target="tpu_custom_call" | custom-call | flops 471859200 | bytes 262144 | tf_op jit(solution)/shard_map/pallas_call | solution.py:197
  23.7 0.0 collective-permute-done.below_ref
  23.8 0.0 collective-permute-done.1.above_ref
  23.8 0.0 copy-done.1
  23.8 0.0 copy-done.2
  23.8 4.5 %shard_map.61 = (f32[2,4,256]{2,1,0:T(4,128)S(1)}, f32[2,4,256]{2,1,0:T(4,128)S(1)}) custom-call(s32[1,1,2]{2,1,0:T(1,128)S(1)} %copy-done.1, f32[3,1,1,2,256]{4,3,2,1,0:T(2,128)S(1)} %copy-done.2, f32[2,4,256]{2,1,0:T(4,128)S(1)} %copy-done, f32[2,32,256]{2,1,0:T(8,128)S(1)} %shard_map.60.total_ref, f32[8,4,256]{2,1,0:T(4,128)S(1)} %collective-permute-done.below_ref, ...), custom_call_target="tpu_custom_call" | custom-call | flops 235929600 | bytes 262144 | tf_op jit(solution)/shard_map/pallas_call | solution.py:206
  28.3 7.1 %all_to_all.11 = f32[2,8,4,256]{3,2,0,1:T(4,128)S(1)} all-to-all(f32[2,8,4,256]{3,2,0,1:T(4,128)S(1)} %broadcast_in_dim.5), channel_id=1, replica_groups=mesh['gx'=4,'gy'=2,'gz'=4] {'gx','gy'}, dimensions={1} | all-to-all | bytes 131072 | tf_op jit(solution)/shard_map/all_to_all | solution.py:193
  35.5 0.0 collective-permute-start.2
  35.5 3.8 %collective-permute-start.3 = (f32[8,4,256]{2,1,0:T(4,128)S(1)}, f32[8,4,256]{2,1,0:T(4,128)S(1)}, u32[]{:S(2)}, u32[]{:S(2)}) collective-permute-start(f32[8,4,256]{2,1,0:T(4,128)S(1)} %get-tuple-element.7.low_ref), channel_id=1, source_target_pairs={{0,3},{1,0},{2,1},{3,2},{4,7},{5,4},{6,5},{7,6},{8,11},{9,8},{10,9... | collective-permute-start | bytes 98312 | tf_op jit(solution)/shard_map/ppermute | solution.py:196
  39.3 7.4 %shard_map.62.total_ref = f32[2,32,256]{2,1,0:T(8,128)S(1)} custom-call(f32[2,4,256]{2,1,0:T(4,128)S(1)} %get-tuple-element.5.own_ref, f32[8,4,256]{2,1,0:T(4,128)S(1)} %get-tuple-element.7.low_ref, f32[8,4,256]{2,1,0:T(4,128)S(1)} %get-tuple-element.6.high_ref), custom_call_target="tpu_custom_call" | custom-call | flops 471859200 | bytes 262144 | tf_op jit(solution)/shard_map/pallas_call | solution.py:197
  46.7 0.0 collective-permute-done.2.below_ref
  46.8 0.0 collective-permute-done.3.above_ref
  46.8 5.1 %shard_map.63 = (f32[3,1,1,2,256]{4,3,2,1,0:T(2,128)}, f32[3,1,1,2,256]{4,3,2,1,0:T(2,128)}) custom-call(s32[1,1,2]{2,1,0:T(1,128)S(1)} %copy-done.1, f32[2,4,256]{2,1,0:T(4,128)S(1)} %get-tuple-element.4.speed_ref, f32[2,4,256]{2,1,0:T(4,128)S(1)} %get-tuple-element.5.own_ref, f32[2,32,256]{2,1,0:T(8,128)S(1)} %shard_map.62.total_ref, ...), custom_call_target="tpu_custom_call" | custom-call | flops 235929600 | bytes 262144 | tf_op jit(solution)/shard_map/pallas_call | solution.py:206
  (3 shorter events, 0.0 us)
Async XLA Ops:
  12.4 3.9 %copy-start = (f32[2,4,256]{2,1,0:T(4,128)S(1)}, f32[2,4,256]{2,1,0:T(4,128)}, u32[]{:S(2)}) copy-start(f32[2,4,256]{2,1,0:T(4,128)} %shard_map.59.own_ref) | copy-start | bytes 24580
  12.4 11.4 %collective-permute-start = (f32[8,4,256]{2,1,0:T(4,128)S(1)}, f32[8,4,256]{2,1,0:T(4,128)S(1)}, u32[]{:S(2)}, u32[]{:S(2)}) collective-permute-start(f32[8,4,256]{2,1,0:T(4,128)S(1)} %get-tuple-element.8.high_ref), channel_id=1, source_target_pairs={{0,1},{1,2},{2,3},{3,0},{4,5},{5,6},{6,7},{7,4},{8,9},{9,10},{10,1... | collective-permute-start | bytes 98312 | tf_op jit(solution)/shard_map/ppermute | solution.py:195
  14.0 9.8 %copy-start.1 = (s32[1,1,2]{2,1,0:T(1,128)S(1)}, s32[1,1,2]{2,1,0:T(1,128)}, u32[]{:S(2)}) copy-start(s32[1,1,2]{2,1,0:T(1,128)} %counts_ref.5) | copy-start | bytes 28
  14.0 9.8 %copy-start.2 = (f32[3,1,1,2,256]{4,3,2,1,0:T(2,128)S(1)}, f32[3,1,1,2,256]{4,3,2,1,0:T(2,128)}, u32[]{:S(2)}) copy-start(f32[3,1,1,2,256]{4,3,2,1,0:T(2,128)} %speed_ref.1) | copy-start | bytes 18436
  14.0 9.7 %collective-permute-start.1 = (f32[8,4,256]{2,1,0:T(4,128)S(1)}, f32[8,4,256]{2,1,0:T(4,128)S(1)}, u32[]{:S(2)}, u32[]{:S(2)}) collective-permute-start(f32[8,4,256]{2,1,0:T(4,128)S(1)} %get-tuple-element.9.low_ref), channel_id=1, source_target_pairs={{0,3},{1,0},{2,1},{3,2},{4,7},{5,4},{6,5},{7,6},{8,11},{9,8},{10,9... | collective-permute-start | bytes 98312 | tf_op jit(solution)/shard_map/ppermute | solution.py:196
  35.5 11.3 %collective-permute-start.2 = (f32[8,4,256]{2,1,0:T(4,128)S(1)}, f32[8,4,256]{2,1,0:T(4,128)S(1)}, u32[]{:S(2)}, u32[]{:S(2)}) collective-permute-start(f32[8,4,256]{2,1,0:T(4,128)S(1)} %get-tuple-element.6.high_ref), channel_id=1, source_target_pairs={{0,1},{1,2},{2,3},{3,0},{4,5},{5,6},{6,7},{7,4},{8,9},{9,10},{10,1... | collective-permute-start | bytes 98312 | tf_op jit(solution)/shard_map/ppermute | solution.py:195
  35.5 11.3 %collective-permute-start.3 = (f32[8,4,256]{2,1,0:T(4,128)S(1)}, f32[8,4,256]{2,1,0:T(4,128)S(1)}, u32[]{:S(2)}, u32[]{:S(2)}) collective-permute-start(f32[8,4,256]{2,1,0:T(4,128)S(1)} %get-tuple-element.7.low_ref), channel_id=1, source_target_pairs={{0,3},{1,0},{2,1},{3,2},{4,7},{5,4},{6,5},{7,6},{8,11},{9,8},{10,9... | collective-permute-start | bytes 98312 | tf_op jit(solution)/shard_map/ppermute | solution.py:196
where the time goes:
time: 52.2 us; the launch traced here: 51.9 us
  Pallas kernels  25.8 us (49%)
  blocking collectives  16.9 us (32%)
  starting transfers between devices  7.69 us (15%)
  local copies, waits for them, and re-layouts  0.74 us (1%)
  between operations  0.71 us (1%)
    all_to_all x2, blocking collectives, on_device(): planes = lax.all_to_all(copies, ('gx', 'gy'), 1, 1, tiled=True)  16.9 us
    pallas_call x2, Pallas kernels, on_device(): pl.pallas_call(functools.partial(inner_kernel, sizes), out_shape=jax.Shap...  14.9 us
    pallas_call x2, Pallas kernels, on_device(): pl.pallas_call(functools.partial(outer_kernel, sizes, first, last), out_s...  9.64 us
    ppermute x2, starting transfers between devices, on_device(): above = lax.ppermute(low, 'gz', ring('gz', -1))  6.06 us
    ppermute x2, starting transfers between devices, on_device(): below = lax.ppermute(high, 'gz', ring('gz', 1))  1.63 us
    pallas_call x1, Pallas kernels, on_device(): pl.pallas_call(pack_kernel, out_shape=bins, in_specs=[SMEM, VMEM, VMEM],...  1.31 us
  transfers between devices with their start and end apart: 4, of which 0 were waited for; matrix products, arithmetic and copies ran while one was open for 0% of the time, Pallas kernels for 29%

commit v1 on v0

--- a/solution.py
+++ b/solution.py
@@ -91,10 +91,12 @@
     return places
 
 
-def fill(refs, levels, sizes, near_ref, sum_ref):
-    for column, (place, x, y) in enumerate(gather_column(*sizes)):
-        for slot, (ref, level) in enumerate(zip(refs, levels)):
-            distance, summed = source_rows(ref[place], (x, y, level - CENTRE[2]))
+def fill(gathered_ref, sizes, near_ref, sum_ref):
+    here, size = lax.axis_index("gz"), sizes[2]
+    levels = ((lax.rem(here + (size - 1), size), 1), (here, 0), (here, 1), (lax.rem(here + 1, size), 0))
+    for column, (place, x, y) in enumerate(gather_column(sizes[0], sizes[1])):
+        for slot, (device, z) in enumerate(levels):
+            distance, summed = source_rows(gathered_ref[place * size + device, z], (x, y, slot - 1 - CENTRE[2]))
             near_ref[column, slot] = distance
             sum_ref[column, slot] = summed
 
@@ -119,26 +121,17 @@
     return lax.fori_loop(0, near_ref.shape[0], column_step, tuple(totals))
 
 
-def inner_kernel(sizes, own_ref, low_ref, high_ref, total_ref, near_ref, sum_ref):
-    _, moved = target_places(own_ref)
-    targets = [target_rows(m) for m in moved]
-    fill((low_ref, high_ref), (0, 1), sizes, near_ref, sum_ref)
-    zero = jnp.zeros(total_ref.shape[1:], F32)
-    totals = totals_over(targets, ((0, 1), (0, 1)), near_ref, sum_ref, (zero, zero))
-    for z in range(2):
-        total_ref[z] = totals[z]
-
-
-def outer_kernel(sizes, first, last, counts_ref, speed_ref, own_ref, total_ref, below_ref, above_ref, *refs):
+def step_kernel(sizes, first, last, counts_ref, speed_ref, own_ref, gathered_ref, *refs):
     if last:
         place_out, speed_out, near_ref, sum_ref = refs
     else:
         packed_out, speed_out, near_ref, sum_ref = refs
     own, moved = target_places(own_ref)
     targets = [target_rows(m) for m in moved]
-    fill((below_ref, above_ref), (-1, 2), sizes, near_ref, sum_ref)
-    totals = totals_over(targets, ((0,), (1,)), near_ref, sum_ref, (total_ref[0], total_ref[1]))
+    fill(gathered_ref, sizes, near_ref, sum_ref)
     slots = own[0].shape[-1]
+    zero = jnp.zeros((32, slots), F32)
+    totals = totals_over(targets, ((0, 1, 2), (1, 2, 3)), near_ref, sum_ref, (zero, zero))
     for z in range(2):
         total = totals[z][0:8] + totals[z][8:16] + totals[z][16:24]
         total = total[0:4]
@@ -165,19 +158,13 @@
 PARAMS = pltpu.CompilerParams(vmem_limit_bytes=32 * 1024 * 1024)
 
 
-def ring(axis, step):
-    size = lax.axis_size(axis)
-    return [(i, (i + step) % size) for i in range(size)]
-
-
 def cost(pairs, slots):
     return pl.CostEstimate(flops=pairs * slots * slots * 200, bytes_accessed=1 << 18, transcendentals=0)
 
 
 def on_device(positions, velocities, mass, counts):
     slots = positions.shape[-1]
-    sizes = (lax.axis_size("gx"), lax.axis_size("gy"))
-    columns = sizes[0] * sizes[1]
+    sizes = (lax.axis_size("gx"), lax.axis_size("gy"), lax.axis_size("gz"))
     bins = jax.ShapeDtypeStruct((2, 4, slots), F32)
     full = jax.ShapeDtypeStruct(positions.shape, F32)
     packed = pl.pallas_call(
@@ -189,29 +176,16 @@
     speed = velocities
     for subcycle in range(SUBCYCLES):
         first, last = subcycle == 0, subcycle == SUBCYCLES - 1
-        copies = jnp.broadcast_to(packed[:, None], (2, columns, 4, slots))
-        planes = lax.all_to_all(copies, ("gx", "gy"), 1, 1, tiled=True)
-        low, high = planes[0], planes[1]
-        below = lax.ppermute(high, "gz", ring("gz", 1))
-        above = lax.ppermute(low, "gz", ring("gz", -1))
-        total = pl.pallas_call(
-            functools.partial(inner_kernel, sizes),
-            out_shape=jax.ShapeDtypeStruct((2, 32, slots), F32),
-            in_specs=[VMEM] * 3,
-            out_specs=VMEM,
-            scratch_shapes=[pltpu.VMEM((9, 2, 48, slots), BF16), pltpu.VMEM((9, 2, 32, slots), BF16)],
+        gathered = lax.all_gather(packed, ("gx", "gy", "gz"), tiled=False)
+        packed, speed = pl.pallas_call(
+            functools.partial(step_kernel, sizes, first, last),
+            out_shape=(full, full) if last else (bins, bins),
+            in_specs=[SMEM] + [VMEM] * 3,
+            out_specs=(VMEM, VMEM),
+            scratch_shapes=[pltpu.VMEM((9, 4, 48, slots), BF16), pltpu.VMEM((9, 4, 32, slots), BF16)],
             compiler_params=PARAMS,
-            cost_estimate=cost(36, slots),
-        )(packed, low, high)
-        packed, speed = pl.pallas_call(
-            functools.partial(outer_kernel, sizes, first, last),
-            out_shape=(full, full) if last else (bins, bins),
-            in_specs=[SMEM] + [VMEM] * 5,
-            out_specs=(VMEM, VMEM),
-            scratch_shapes=[pltpu.VMEM((9, 2, 48, slots), BF16), pltpu.VMEM((9, 2, 32, slots), BF16)],
-            compiler_params=PARAMS,
-            cost_estimate=cost(18, slots),
-        )(counts, speed, packed, total, below, above)
+            cost_estimate=cost(54, slots),
+        )(counts, speed, packed, gathered)
     return packed, speed
 
 

time: 52.2 us -> 162 us (3.10)
  blocking collectives: 16.9 us -> 138 us
  starting transfers between devices: 7.69 us -> 0 us
  Pallas kernels: 25.8 us -> 23.1 us
    all_gather x0 -> x2, blocking collectives: none -> 138 us  [on_device(): gathered = lax.all_gather(packed, ('gx', 'gy', 'gz'), tiled=False)]
    all_to_all x2 -> x0, blocking collectives: 16.9 us -> none  [on_device(): planes = lax.all_to_all(copies, ('gx', 'gy'), 1, 1, tiled=True)]
    ppermute x4 -> x0, starting transfers between devices: 7.69 us -> none  [the longest x2 6.06 us: on_device(): above = lax.ppermute(low, 'gz', ring('gz', -1))]
    pallas_call x4 -> x2, Pallas kernels: 24.5 us -> 21.8 us  [on_device(): pl.pallas_call(functools.partial(step_kernel, sizes, first, last), out_sh...]
  transfers between devices with their start and end apart: 4 -> 0, of which waited for: 0 -> 0; matrix products, arithmetic and copies ran while one was open for 0% -> 0% of each run, Pallas kernels for 29% -> 0%
where the time goes in v1:
time: 162 us
  blocking collectives  138 us (85%)
  Pallas kernels  23.1 us (14%)
    all_gather x2, blocking collectives, on_device(): gathered = lax.all_gather(packed, ('gx', 'gy', 'gz'), tiled=False)  138 us
    pallas_call x2, Pallas kernels, on_device(): pl.pallas_call(functools.partial(step_kernel, sizes, first, last), out_sh...  21.8 us

profile of v1, /device:TPU:0, one launch (start us, length us, event | category | flops | bytes accessed | tf_op | source)
XLA Modules:
  0.0 162.3 jit_solution(205802290219619276)
XLA Ops:
  0.6 1.3 shard_map.59.own_ref
  1.9 0.0 copy-start
  1.9 0.0 copy-start.2
  1.9 72.2 %all-gather = f32[64,4,256]{2,1,0:T(4,128)S(1)} all-gather(f32[2,4,256]{2,1,0:T(4,128)} %shard_map.59.own_ref), channel_id=2, replica_groups=mesh['gx'=4,'gy'=2,'gz'=4] {'gx','gy','gz'}, dimensions={0}, use_global_device_ids=true | all-gather | bytes 270336 | tf_op jit(solution)/shard_map/all_gather | solution.py:179
  74.2 0.0 copy-start.1
  74.2 0.0 copy-done
  74.2 0.0 copy-done.2
  74.2 0.6 copy-done.1
  74.9 10.6 %shard_map.60 = (f32[2,4,256]{2,1,0:T(4,128)S(1)}, f32[2,4,256]{2,1,0:T(4,128)S(1)}) custom-call(s32[1,1,2]{2,1,0:T(1,128)S(1)} %copy-done.1, f32[3,1,1,2,256]{4,3,2,1,0:T(2,128)S(1)} %copy-done.2, f32[2,4,256]{2,1,0:T(4,128)S(1)} %copy-done, f32[32,2,4,256]{3,2,1,0:T(4,128)S(1)} %bitcast.3), custom_call_target="tpu_custom_call" | custom-call | flops 707788800 | bytes 262144 | tf_op jit(solution)/shard_map/pallas_call | solution.py:180
  85.5 65.6 %all-gather.1 = f32[64,4,256]{2,1,0:T(4,128)S(1)} all-gather(f32[2,4,256]{2,1,0:T(4,128)S(1)} %get-tuple-element.5.own_ref), channel_id=3, replica_groups=mesh['gx'=4,'gy'=2,'gz'=4] {'gx','gy','gz'}, dimensions={0}, use_global_device_ids=true | all-gather | bytes 270336 | tf_op jit(solution)/shard_map/all_gather | solution.py:179
  151.0 11.2 %shard_map.61 = (f32[3,1,1,2,256]{4,3,2,1,0:T(2,128)}, f32[3,1,1,2,256]{4,3,2,1,0:T(2,128)}) custom-call(s32[1,1,2]{2,1,0:T(1,128)S(1)} %copy-done.1, f32[2,4,256]{2,1,0:T(4,128)S(1)} %get-tuple-element.4.speed_ref, f32[2,4,256]{2,1,0:T(4,128)S(1)} %get-tuple-element.5.own_ref, f32[32,2,4,256]{3,2,1,0:T(4,128)S(1)} %bitcast.2), custom_call_target="tpu_custom_call" | custom-call | flops 707788800 | bytes 262144 | tf_op jit(solution)/shard_map/pallas_call | solution.py:180
Async XLA Ops:
  1.9 72.3 %copy-start = (f32[2,4,256]{2,1,0:T(4,128)S(1)}, f32[2,4,256]{2,1,0:T(4,128)}, u32[]{:S(2)}) copy-start(f32[2,4,256]{2,1,0:T(4,128)} %shard_map.59.own_ref) | copy-start | bytes 24580
  1.9 72.3 %copy-start.2 = (f32[3,1,1,2,256]{4,3,2,1,0:T(2,128)S(1)}, f32[3,1,1,2,256]{4,3,2,1,0:T(2,128)}, u32[]{:S(2)}) copy-start(f32[3,1,1,2,256]{4,3,2,1,0:T(2,128)} %speed_ref.1) | copy-start | bytes 18436
  74.2 0.7 copy-start.1

commit v2 on v1

v2 whole, which is shorter than its diff:
```python
import functools

import jax
import jax.numpy as jnp
from jax import lax
from jax.experimental import pallas as pl
from jax.experimental.pallas import tpu as pltpu
from jax.sharding import PartitionSpec as P

SUBCYCLES = 2

time_step = 0.25

CENTRE = (0.5, 0.5, 1.0)
F32, BF16 = jnp.float32, jnp.bfloat16


def parts(value):
    high = value.astype(BF16).astype(F32)
    rest = value - high
    mid = rest.astype(BF16).astype(F32)
    return high, mid, rest - mid


def row_index(rows, slots):
    return lax.broadcasted_iota(jnp.int32, (rows, slots), 0)


def shifted(packed, offset):
    row = row_index(*packed.shape)
    x, y, z = [jnp.asarray(o, F32) - c for o, c in zip(offset, CENTRE)]
    move = jnp.where(row == 0, x, jnp.where(row == 1, y, jnp.where(row == 2, z, 0.0)))
    return packed + move


def source_rows(packed, offset):
    slots = packed.shape[-1]
    moved = shifted(packed, offset)
    row = row_index(4, slots)
    square = jnp.sum(jnp.where(row < 3, moved * moved, 0.0), axis=0, keepdims=True)
    head = jnp.where(row < 3, moved, square)
    tail = jnp.where(row == 0, 1.0, 0.0).astype(F32)
    high, mid, low = parts(jnp.concatenate([head, tail], axis=0))
    distance = jnp.concatenate([high, high, high, mid, mid, low], axis=0).astype(BF16)
    mass = moved[3:4]
    carried = jnp.where(row < 3, moved * mass, mass)
    high, mid, low = parts(jnp.concatenate([carried, jnp.zeros_like(carried)], axis=0))
    summed = jnp.concatenate([high, mid, low, jnp.zeros_like(low)], axis=0).astype(BF16)
    return distance, summed


def target_rows(moved):
    slots = moved.shape[-1]
    row = row_index(4, slots)
    square = jnp.sum(jnp.where(row < 3, moved * moved, 0.0), axis=0, keepdims=True)
    head = jnp.where(row < 3, 2.0 * moved, -1.0)
    tail = jnp.where(row == 0, 1.0 - square, 0.0)
    high, mid, low = parts(jnp.concatenate([head, tail], axis=0))
    return jnp.concatenate([high, mid, low, high, mid, high], axis=0).T.astype(BF16)


def pair_weight(target, source):
    near = jnp.maximum(jnp.dot(target, source, preferred_element_type=F32), 0.0)
    weight = near * near * near
    high = weight.astype(BF16)
    return high, (weight - high.astype(F32)).astype(BF16)


def contract(weights, rows):
    return lax.dot_general(weights, rows, (((1,), (1,)), ((), ())), preferred_element_type=F32)


def occupied(counts_ref, z, shape):
    return lax.broadcasted_iota(jnp.int32, shape, 1) < counts_ref[0, 0, z]


def pack_kernel(counts_ref, place_ref, mass_ref, packed_ref):
    for z in range(2):
        mass = mass_ref[0, 0, z : z + 1, :]
        weight = jnp.where(occupied(counts_ref, z, mass.shape), mass, 0.0)
        rows = [place_ref[c, 0, 0, z : z + 1, :] for c in range(3)]
        packed_ref[z] = jnp.concatenate(rows + [weight], axis=0)


def ahead(axis):
    return 1 - 2 * lax.rem(lax.axis_index(axis), 2)


def y_shifts(size):
    if size == 2:
        return [[0], [-1, 1]]
    return [[0], [ahead("gy")], [-ahead("gy")]]


def fill(near_ref, sum_ref, entries):
    for number, (packed, offset) in enumerate(entries):
        group, member = divmod(number, 3)
        distance, summed = source_rows(packed, offset)
        near_ref[group, member] = distance
        sum_ref[group, member] = summed


def gathered(target, near_ref, sum_ref, group, members):
    highs, lows, rows = [], [], []
    for member in members:
        high, low = pair_weight(target, near_ref[group, member])
        highs.append(high)
        lows.append(low)
        rows.append(sum_ref[group, member])
    rows = jnp.concatenate(rows, axis=1)
    return contract(jnp.concatenate(highs + lows, axis=1), jnp.concatenate([rows, rows], axis=1))


def both_targets(target_ref, near_ref, sum_ref, totals):
    targets = [target_ref[z] for z in range(2)]

    def step(group, totals):
        return tuple(totals[z] + gathered(targets[z], near_ref, sum_ref, group, range(3)) for z in range(2))

    return lax.fori_loop(0, near_ref.shape[0], step, tuple(totals))


def plane_kernel(size_y, *refs):
    planes, (target_ref, total_ref, near_ref, sum_ref) = refs[:-4], refs[-4:]
    own_ref = planes[0]
    for z in range(2):
        target_ref[z] = target_rows(shifted(own_ref[z], (0, 0, z)))
    entries = []
    for ref, shifts in zip(planes, y_shifts(size_y)):
        for y in shifts:
            entries += [(ref[z], (0, y, z)) for z in range(2)]
    fill(near_ref, sum_ref, entries)
    zero = jnp.zeros(total_ref.shape[1:], F32)
    totals = both_targets(target_ref, near_ref, sum_ref, (zero, zero))
    for z in range(2):
        total_ref[z] = totals[z]


def slab_kernel(size_y, target_ref, before_ref, near_x_ref, far_x_ref, total_ref, near_ref, sum_ref):
    entries = []
    for ref, x in ((near_x_ref, ahead("gx")), (far_x_ref, -ahead("gx"))):
        for plane, shifts in enumerate(y_shifts(size_y)):
            for y in shifts:
                entries += [(ref[plane, z], (x, y, z)) for z in range(2)]
    fill(near_ref, sum_ref, entries)
    totals = both_targets(target_ref, near_ref, sum_ref, (before_ref[0], before_ref[1]))
    for z in range(2):
        total_ref[z] = totals[z]


def level_kernel(size_y, first, last, counts_ref, speed_ref, own_ref, target_ref, before_ref, near_z_ref, far_z_ref, *refs):
    if last:
        place_out, speed_out, near_ref, sum_ref = refs
    else:
        packed_out, speed_out, near_ref, sum_ref = refs
    turn = ahead("gz")
    near_z = (1 + turn) // 2
    sides = ((near_z_ref, near_z), (far_z_ref, 1 - near_z))
    lists = []
    for ref, z in sides:
        entries = []
        for column, x in enumerate((0, ahead("gx"), -ahead("gx"))):
            for plane, shifts in enumerate(y_shifts(size_y)):
                entries += [(ref[column, plane], (x, y, 3 * z - 1)) for y in shifts]
        lists.append(entries)
    entries = []
    for group in range(3):
        for side in range(2):
            entries += lists[side][3 * group : 3 * group + 3]
    for number, (packed, offset) in enumerate(entries):
        group, member = divmod(number, 6)
        distance, summed = source_rows(packed, offset)
        near_ref[group, member] = distance
        sum_ref[group, member] = summed
    targets = [target_ref[z] for _, z in sides]

    def step(group, totals):
        return tuple(
            totals[side] + gathered(targets[side], near_ref, sum_ref, group, range(3 * side, 3 * side + 3)) for side in range(2)
        )

    totals = lax.fori_loop(0, near_ref.shape[0], step, tuple(before_ref[z] for _, z in sides))
    slots = own_ref.shape[-1]
    swap = near_z == 1
    totals = [total.T for total in totals]
    totals = [jnp.where(swap, totals[1 - z], totals[z]) for z in range(2)]
    for z in range(2):
        total = totals[z][0:8] + totals[z][8:16] + totals[z][16:24]
        total = total[0:4]
        own = own_ref[z]
        accel = total - shifted(own, (0, 0, z)) * total[3:4]
        if first:
            speed = jnp.concatenate([speed_ref[c, 0, 0, z : z + 1, :] for c in range(3)] + [jnp.zeros((1, slots), F32)], axis=0)
        else:
            speed = speed_ref[z]
        speed = speed + time_step * accel
        place = jnp.clip(own + time_step * speed, 0.0, 1.0)
        if last:
            keep = occupied(counts_ref, z, (1, slots))
            for c in range(3):
                place_out[c, 0, 0, z : z + 1, :] = jnp.where(keep, place[c : c + 1], 0.0)
                speed_out[c, 0, 0, z : z + 1, :] = jnp.where(keep, speed[c : c + 1], 0.0)
        else:
            row = row_index(4, slots)
            packed_out[z] = jnp.where(row < 3, place, own)
            speed_out[z] = speed


VMEM = pl.BlockSpec(memory_space=pltpu.VMEM)
SMEM = pl.BlockSpec(memory_space=pltpu.SMEM)


def swaps(axis):
    size = lax.axis_size(axis)
    near = [(i, i ^ 1) for i in range(size)]
    far = [(i, (((i + 1) ^ 1) - 1) % size) for i in range(size)]
    return near, far


def scratch(groups, members, slots):
    return [pltpu.VMEM((groups, members, 48, slots), BF16), pltpu.VMEM((groups, members, 32, slots), BF16)]


def call(kernel, inputs, outputs, pairs, groups, members, slots):
    return pl.pallas_call(
        kernel,
        out_shape=outputs,
        in_specs=[spec for spec, _ in inputs],
        out_specs=tuple(VMEM for _ in outputs),
        scratch_shapes=scratch(groups, members, slots),
        compiler_params=pltpu.CompilerParams(vmem_limit_bytes=24 * 1024 * 1024),
        cost_estimate=pl.CostEstimate(flops=pairs * slots * slots * 1000, bytes_accessed=1 << 18, transcendentals=0),
    )(*[value for _, value in inputs])


def on_device(positions, velocities, mass, counts):
    slots = positions.shape[-1]
    size_y = lax.axis_size("gy")
    bins = jax.ShapeDtypeStruct((2, 4, slots), F32)
    full = jax.ShapeDtypeStruct(positions.shape, F32)
    running = jax.ShapeDtypeStruct((2, slots, 32), F32)
    packed = pl.pallas_call(
        pack_kernel,
        out_shape=bins,
        in_specs=[SMEM, VMEM, VMEM],
        out_specs=VMEM,
    )(counts, positions, mass)
    speed = velocities
    upper = lax.rem(lax.axis_index("gz"), 2)
    for subcycle in range(SUBCYCLES):
        first, last = subcycle == 0, subcycle == SUBCYCLES - 1
        near, far = swaps("gy")
        planes = [packed]
        if size_y > 2:
            other = lax.ppermute(packed, "gy", far)
            planes += [lax.ppermute(packed, "gy", near), other]
        else:
            planes.append(lax.ppermute(packed, "gy", near))
        plane = jnp.stack(planes)
        near, far = swaps("gx")
        far_x = lax.ppermute(plane, "gx", far)
        near_x = lax.ppermute(plane, "gx", near)
        targets, total = call(
            functools.partial(plane_kernel, size_y),
            [(VMEM, value) for value in planes],
            (jax.ShapeDtypeStruct((2, slots, 48), BF16), running),
            12, 2, 3, slots,
        )
        slab = jnp.stack([plane, near_x, far_x])
        near, far = swaps("gz")
        far_z = lax.ppermute(lax.dynamic_index_in_dim(slab, upper, 2, False), "gz", far)
        near_z = lax.ppermute(lax.dynamic_index_in_dim(slab, 1 - upper, 2, False), "gz", near)
        (total,) = call(
            functools.partial(slab_kernel, size_y),
            [(VMEM, value) for value in (targets, total, near_x, far_x)],
            (running,),
            24, 4, 3, slots,
        )
        packed, speed = call(
            functools.partial(level_kernel, size_y, first, last),
            [(SMEM, counts)] + [(VMEM, value) for value in (speed, packed, targets, total, near_z, far_z)],
            (full, full) if last else (bins, bins),
            18, 3, 6, slots,
        )
    return packed, speed


def solution(mesh):
    placed = (
        P(None, "gx", "gy", "gz", None),
        P(None, "gx", "gy", "gz", None),
        P("gx", "gy", "gz", None),
        P("gx", "gy", "gz"),
    )
    return jax.shard_map(
        on_device,
        mesh=mesh,
        in_specs=placed,
        out_specs=(P(None, "gx", "gy", "gz", None), P(None, "gx", "gy", "gz", None)),
        check_vma=False,
    )
```

time: 162 us -> 39.5 us (0.24)
  blocking collectives: 138 us -> 0 us
  starting transfers between devices: 0 us -> 14.4 us
  waiting for transfers between devices: 0 us -> 4.65 us
  Pallas kernels: 23.1 us -> 19.4 us
    all_gather x2 -> x0, blocking collectives: 138 us -> none  [on_device(): gathered = lax.all_gather(packed, ('gx', 'gy', 'gz'), tiled=False)]
    ppermute x0 -> x10, starting transfers between devices: none -> 14.4 us  [the longest x2 4.54 us: on_device(): planes.append(lax.ppermute(packed, 'gy', near))]
    ppermute x0 -> x10, waiting for transfers between devices: none -> 4.65 us  [the longest x2 3.98 us: on_device(): planes.append(lax.ppermute(packed, 'gy', near))]
    pallas_call x2 -> x6, Pallas kernels: 21.8 us -> 18 us  [call(): pl.pallas_call(kernel, out_shape=outputs, in_specs=[spec for spec, _ in i...]
  transfers between devices with their start and end apart: 0 -> 10, of which waited for: 0 -> 3; matrix products, arithmetic and copies ran while one was open for 0% -> 0% of each run, Pallas kernels for 0% -> 27%
where the time goes in v2:
time: 39.5 us; the launch traced here: 39.3 us
  Pallas kernels  19.4 us (49%)
  starting transfers between devices  14.4 us (36%)
  waiting for transfers between devices  4.65 us (12%)
  between operations  0.78 us (2%)
    pallas_call x6, Pallas kernels, call(): pl.pallas_call(kernel, out_shape=outputs, in_specs=[spec for spec, _ in i...  18 us
    ppermute x2, starting transfers between devices, on_device(): planes.append(lax.ppermute(packed, 'gy', near))  4.54 us
    ppermute x2, waiting for transfers between devices, on_device(): planes.append(lax.ppermute(packed, 'gy', near))  3.98 us
    ppermute x2, starting transfers between devices, on_device(): lax.ppermute(lax.dynamic_index_in_dim(slab, upper, 2, False), 'gz', far)  3.97 us
    ppermute x2, starting transfers between devices, on_device(): far_x = lax.ppermute(plane, 'gx', far)  3.43 us
    ppermute x2, starting transfers between devices, on_device(): lax.ppermute(lax.dynamic_index_in_dim(slab, 1 - upper, 2, False), 'gz', n...  2.37 us
    pallas_call x1, Pallas kernels, on_device(): pl.pallas_call(pack_kernel, out_shape=bins, in_specs=[SMEM, VMEM, VMEM],...  1.31 us
  transfers between devices with their start and end apart: 10, of which 3 were waited for; matrix products, arithmetic and copies ran while one was open for 0% of the time, Pallas kernels for 27%

profile of v2, /device:TPU:0, one launch (start us, length us, event | category | flops | bytes accessed | tf_op | source)
XLA Modules:
  0.0 39.3 jit_solution(7049146776422986632)
XLA Ops:
  0.6 1.3 %shard_map.59.refs_0_.own_ref = f32[2,4,256]{2,1,0:T(4,128)} custom-call(s32[1,1,2]{2,1,0:T(1,128)} %counts_ref.5, f32[3,1,1,2,256]{4,3,2,1,0:T(2,128)} %place_ref.1, f32[1,1,2,256]{3,2,1,0:T(2,128)} %mass_ref.1), custom_call_target="tpu_custom_call" | custom-call | tf_op jit(solution)/shard_map/pallas_call | solution.py:242
  1.9 3.0 %collective-permute-start = (f32[2,4,256]{2,1,0:T(4,128)}, f32[2,4,256]{2,1,0:T(4,128)S(1)}, u32[]{:S(2)}, u32[]{:S(2)}) collective-permute-start(f32[2,4,256]{2,1,0:T(4,128)} %shard_map.59.refs_0_.own_ref), channel_id=1, source_target_pairs={{0,4},{4,0},{1,5},{5,1},{2,6},{6,2},{3,7},{7,3},{8,12},{12,8},{9,1... | collective-permute-start | bytes 24584 | tf_op jit(solution)/shard_map/ppermute | solution.py:258
  4.9 0.0 copy-start
  4.9 1.8 %collective-permute-done.refs_1_ = f32[2,4,256]{2,1,0:T(4,128)S(1)} collective-permute-done((f32[2,4,256]{2,1,0:T(4,128)}, f32[2,4,256]{2,1,0:T(4,128)S(1)}, u32[]{:S(2)}, u32[]{:S(2)}) %collective-permute-start) | collective-permute-done | bytes 8224 | tf_op jit(solution)/shard_map/ppermute | solution.py:258
  6.7 0.0 copy-done
  6.8 0.1 collective-permute-start.1
  6.8 2.1 %collective-permute-start.2 = (f32[2,2,4,256]{3,2,1,0:T(4,128)S(1)}, f32[2,2,4,256]{3,2,1,0:T(4,128)S(1)}, u32[]{:S(2)}, u32[]{:S(2)}) collective-permute-start(f32[2,2,4,256]{3,2,1,0:T(4,128)S(1)} %get-tuple-element.21), channel_id=1, source_target_pairs={{0,24},{8,16},{16,8},{24,0},{1,25},{9,17},{17,9},{25,1},{2,26},{10... | collective-permute-start | bytes 49160 | tf_op jit(solution)/shard_map/ppermute | solution.py:261
  8.9 1.9 %shard_map.60 = (bf16[2,256,48]{2,1,0:T(8,128)(2,1)S(1)}, f32[2,256,32]{2,1,0:T(8,128)S(1)}) custom-call(f32[2,4,256]{2,1,0:T(4,128)S(1)} %copy-done, f32[2,4,256]{2,1,0:T(4,128)S(1)} %collective-permute-done.refs_1_), custom_call_target="tpu_custom_call" | custom-call | flops 786432000 | bytes 262144 | tf_op jit(solution)/shard_map/pallas_call | solution.py:225
  10.8 0.0 collective-permute-done.1.near_x_ref
  10.8 0.0 collective-permute-done.2.far_x_ref
  10.9 1.6 %collective-permute-start.3 = (f32[3,2,4,256]{3,2,1,0:T(4,128)S(1)}, f32[3,2,4,256]{3,2,1,0:T(4,128)S(1)}, u32[]{:S(2)}, u32[]{:S(2)}) collective-permute-start(f32[3,2,4,256]{3,2,1,0:T(4,128)S(1)} %get-tuple-element.17), channel_id=1, source_target_pairs={{0,1},{1,0},{2,3},{3,2},{4,5},{5,4},{6,7},{7,6},{8,9},{9,8},{10,11... | collective-permute-start | bytes 73736 | tf_op jit(solution)/shard_map/ppermute | solution.py:272
  12.5 2.5 %collective-permute-start.4 = (f32[3,2,4,256]{3,2,1,0:T(4,128)S(1)}, f32[3,2,4,256]{3,2,1,0:T(4,128)S(1)}, u32[]{:S(2)}, u32[]{:S(2)}) collective-permute-start(f32[3,2,4,256]{3,2,1,0:T(4,128)S(1)} %get-tuple-element.16), channel_id=1, source_target_pairs={{0,3},{1,2},{2,1},{3,0},{4,7},{5,6},{6,5},{7,4},{8,11},{9,10},{10,... | collective-permute-start | bytes 73736 | tf_op jit(solution)/shard_map/ppermute | solution.py:271
  15.0 0.0 copy-start.1
  15.0 0.0 copy-start.2
  15.0 3.5 %shard_map.61.before_ref = f32[2,256,32]{2,1,0:T(8,128)S(1)} custom-call(bf16[2,256,48]{2,1,0:T(8,128)(2,1)S(1)} %get-tuple-element.8.target_ref, f32[2,256,32]{2,1,0:T(8,128)S(1)} %get-tuple-element.9.before_ref, f32[2,2,4,256]{3,2,1,0:T(4,128)S(1)} %collective-permute-done.1.near_x_ref, f32[2,2,4,256]{3,2,1,0:T(4,128)S(1)} %collective-permute-done.2.far_x_ref), custom_call_target="tpu_custom_call" | custom-call | flops 1572864000 | bytes 262144 | tf_op jit(solution)/shard_map/pallas_call | solution.py:225
  18.5 0.0 collective-permute-done.3.near_z_ref
  18.5 0.0 collective-permute-done.4.far_z_ref
  18.5 0.0 copy-done.1
  18.5 0.0 copy-done.2
  18.5 3.4 %shard_map.62 = (f32[2,4,256]{2,1,0:T(4,128)S(1)}, f32[2,4,256]{2,1,0:T(4,128)S(1)}) custom-call(s32[1,1,2]{2,1,0:T(1,128)S(1)} %copy-done.1, f32[3,1,1,2,256]{4,3,2,1,0:T(2,128)S(1)} %copy-done.2, f32[2,4,256]{2,1,0:T(4,128)S(1)} %copy-done, bf16[2,256,48]{2,1,0:T(8,128)(2,1)S(1)} %get-tuple-element.8.target_ref, f32[2,256,32]{2,1,0:T(8,128)S(1)} %shard_map.61.before_ref, ...), custom_call_target="tpu_custom_call" | custom-call | flops 1179648000 | bytes 262144 | tf_op jit(solution)/shard_map/pallas_call | solution.py:225
  21.9 1.6 %collective-permute-start.5 = (f32[2,4,256]{2,1,0:T(4,128)S(1)}, f32[2,4,256]{2,1,0:T(4,128)S(1)}, u32[]{:S(2)}, u32[]{:S(2)}) collective-permute-start(f32[2,4,256]{2,1,0:T(4,128)S(1)} %get-tuple-element.11.refs_0_.own_ref), channel_id=1, source_target_pairs={{0,4},{4,0},{1,5},{5,1},{2,6},{6,2},{3,7},{7,3},{8,12},{12,8},{9,1... | collective-permute-start | bytes 24584 | tf_op jit(solution)/shard_map/ppermute | solution.py:258
  23.5 2.1 %collective-permute-done.5.refs_1_ = f32[2,4,256]{2,1,0:T(4,128)S(1)} collective-permute-done((f32[2,4,256]{2,1,0:T(4,128)S(1)}, f32[2,4,256]{2,1,0:T(4,128)S(1)}, u32[]{:S(2)}, u32[]{:S(2)}) %collective-permute-start.5) | collective-permute-done | bytes 8224 | tf_op jit(solution)/shard_map/ppermute | solution.py:258
  25.7 0.1 collective-permute-start.6
  25.7 1.3 %collective-permute-start.7 = (f32[2,2,4,256]{3,2,1,0:T(4,128)S(1)}, f32[2,2,4,256]{3,2,1,0:T(4,128)S(1)}, u32[]{:S(2)}, u32[]{:S(2)}) collective-permute-start(f32[2,2,4,256]{3,2,1,0:T(4,128)S(1)} %get-tuple-element.19), channel_id=1, source_target_pairs={{0,24},{8,16},{16,8},{24,0},{1,25},{9,17},{17,9},{25,1},{2,26},{10... | collective-permute-start | bytes 49160 | tf_op jit(solution)/shard_map/ppermute | solution.py:261
  27.1 1.9 %shard_map.63 = (bf16[2,256,48]{2,1,0:T(8,128)(2,1)S(1)}, f32[2,256,32]{2,1,0:T(8,128)S(1)}) custom-call(f32[2,4,256]{2,1,0:T(4,128)S(1)} %get-tuple-element.11.refs_0_.own_ref, f32[2,4,256]{2,1,0:T(4,128)S(1)} %collective-permute-done.5.refs_1_), custom_call_target="tpu_custom_call" | custom-call | flops 786432000 | bytes 262144 | tf_op jit(solution)/shard_map/pallas_call | solution.py:225
  28.9 0.0 collective-permute-done.6.near_x_ref
  28.9 0.0 collective-permute-done.7.far_x_ref
  29.0 0.7 %collective-permute-start.8 = (f32[3,2,4,256]{3,2,1,0:T(4,128)S(1)}, f32[3,2,4,256]{3,2,1,0:T(4,128)S(1)}, u32[]{:S(2)}, u32[]{:S(2)}) collective-permute-start(f32[3,2,4,256]{3,2,1,0:T(4,128)S(1)} %get-tuple-element.15), channel_id=1, source_target_pairs={{0,1},{1,0},{2,3},{3,2},{4,5},{5,4},{6,7},{7,6},{8,9},{9,8},{10,11... | collective-permute-start | bytes 73736 | tf_op jit(solution)/shard_map/ppermute | solution.py:272
  29.7 1.5 %collective-permute-start.9 = (f32[3,2,4,256]{3,2,1,0:T(4,128)S(1)}, f32[3,2,4,256]{3,2,1,0:T(4,128)S(1)}, u32[]{:S(2)}, u32[]{:S(2)}) collective-permute-start(f32[3,2,4,256]{3,2,1,0:T(4,128)S(1)} %get-tuple-element.14), channel_id=1, source_target_pairs={{0,3},{1,2},{2,1},{3,0},{4,7},{5,6},{6,5},{7,4},{8,11},{9,10},{10,... | collective-permute-start | bytes 73736 | tf_op jit(solution)/shard_map/ppermute | solution.py:271
  31.2 3.5 %shard_map.64.before_ref = f32[2,256,32]{2,1,0:T(8,128)S(1)} custom-call(bf16[2,256,48]{2,1,0:T(8,128)(2,1)S(1)} %get-tuple-element.12.target_ref, f32[2,256,32]{2,1,0:T(8,128)S(1)} %get-tuple-element.13.before_ref, f32[2,2,4,256]{3,2,1,0:T(4,128)S(1)} %collective-permute-done.6.near_x_ref, f32[2,2,4,256]{3,2,1,0:T(4,128)S(1)} %collective-permute-done.7.far_x_ref), custom_call_target="tpu_custom_call" | custom-call | flops 1572864000 | bytes 262144 | tf_op jit(solution)/shard_map/pallas_call | solution.py:225
  34.7 0.0 collective-permute-done.8.near_z_ref
  34.7 0.6 %collective-permute-done.9.far_z_ref = f32[3,2,4,256]{3,2,1,0:T(4,128)S(1)} collective-permute-done((f32[3,2,4,256]{3,2,1,0:T(4,128)S(1)}, f32[3,2,4,256]{3,2,1,0:T(4,128)S(1)}, u32[]{:S(2)}, u32[]{:S(2)}) %collective-permute-start.9) | collective-permute-done | bytes 24608 | tf_op jit(solution)/shard_map/ppermute | solution.py:271
  35.4 4.0 %shard_map.65 = (f32[3,1,1,2,256]{4,3,2,1,0:T(2,128)}, f32[3,1,1,2,256]{4,3,2,1,0:T(2,128)}) custom-call(s32[1,1,2]{2,1,0:T(1,128)S(1)} %copy-done.1, f32[2,4,256]{2,1,0:T(4,128)S(1)} %get-tuple-element.10.speed_ref, f32[2,4,256]{2,1,0:T(4,128)S(1)} %get-tuple-element.11.refs_0_.own_ref, bf16[2,256,48]{2,1,0:T(8,128)(2,1)S(1)} %get-tuple-element.12.target_ref, ...), custom_call_target="tpu_custom_call" | custom-call | flops 1179648000 | bytes 262144 | tf_op jit(solution)/shard_map/pallas_call | solution.py:225
  (6 shorter events, 0.1 us)
Async XLA Ops:
  1.9 4.8 %collective-permute-start = (f32[2,4,256]{2,1,0:T(4,128)}, f32[2,4,256]{2,1,0:T(4,128)S(1)}, u32[]{:S(2)}, u32[]{:S(2)}) collective-permute-start(f32[2,4,256]{2,1,0:T(4,128)} %shard_map.59.refs_0_.own_ref), channel_id=1, source_target_pairs={{0,4},{4,0},{1,5},{5,1},{2,6},{6,2},{3,7},{7,3},{8,12},{12,8},{9,1... | collective-permute-start | bytes 24584 | tf_op jit(solution)/shard_map/ppermute | solution.py:258
  4.9 1.8 %copy-start = (f32[2,4,256]{2,1,0:T(4,128)S(1)}, f32[2,4,256]{2,1,0:T(4,128)}, u32[]{:S(2)}) copy-start(f32[2,4,256]{2,1,0:T(4,128)} %shard_map.59.refs_0_.own_ref) | copy-start | bytes 24580
  6.8 4.1 %collective-permute-start.1 = (f32[2,2,4,256]{3,2,1,0:T(4,128)S(1)}, f32[2,2,4,256]{3,2,1,0:T(4,128)S(1)}, u32[]{:S(2)}, u32[]{:S(2)}) collective-permute-start(f32[2,2,4,256]{3,2,1,0:T(4,128)S(1)} %get-tuple-element.21), channel_id=1, source_target_pairs={{0,8},{8,0},{16,24},{24,16},{1,9},{9,1},{17,25},{25,17},{2,10},{10... | collective-permute-start | bytes 49160 | tf_op jit(solution)/shard_map/ppermute | solution.py:262
  6.8 4.0 %collective-permute-start.2 = (f32[2,2,4,256]{3,2,1,0:T(4,128)S(1)}, f32[2,2,4,256]{3,2,1,0:T(4,128)S(1)}, u32[]{:S(2)}, u32[]{:S(2)}) collective-permute-start(f32[2,2,4,256]{3,2,1,0:T(4,128)S(1)} %get-tuple-element.21), channel_id=1, source_target_pairs={{0,24},{8,16},{16,8},{24,0},{1,25},{9,17},{17,9},{25,1},{2,26},{10... | collective-permute-start | bytes 49160 | tf_op jit(solution)/shard_map/ppermute | solution.py:261
  10.9 7.6 %collective-permute-start.3 = (f32[3,2,4,256]{3,2,1,0:T(4,128)S(1)}, f32[3,2,4,256]{3,2,1,0:T(4,128)S(1)}, u32[]{:S(2)}, u32[]{:S(2)}) collective-permute-start(f32[3,2,4,256]{3,2,1,0:T(4,128)S(1)} %get-tuple-element.17), channel_id=1, source_target_pairs={{0,1},{1,0},{2,3},{3,2},{4,5},{5,4},{6,7},{7,6},{8,9},{9,8},{10,11... | collective-permute-start | bytes 73736 | tf_op jit(solution)/shard_map/ppermute | solution.py:272
  12.5 6.0 %collective-permute-start.4 = (f32[3,2,4,256]{3,2,1,0:T(4,128)S(1)}, f32[3,2,4,256]{3,2,1,0:T(4,128)S(1)}, u32[]{:S(2)}, u32[]{:S(2)}) collective-permute-start(f32[3,2,4,256]{3,2,1,0:T(4,128)S(1)} %get-tuple-element.16), channel_id=1, source_target_pairs={{0,3},{1,2},{2,1},{3,0},{4,7},{5,6},{6,5},{7,4},{8,11},{9,10},{10,... | collective-permute-start | bytes 73736 | tf_op jit(solution)/shard_map/ppermute | solution.py:271
  15.0 3.5 %copy-start.1 = (s32[1,1,2]{2,1,0:T(1,128)S(1)}, s32[1,1,2]{2,1,0:T(1,128)}, u32[]{:S(2)}) copy-start(s32[1,1,2]{2,1,0:T(1,128)} %counts_ref.5) | copy-start | bytes 28
  15.0 3.5 %copy-start.2 = (f32[3,1,1,2,256]{4,3,2,1,0:T(2,128)S(1)}, f32[3,1,1,2,256]{4,3,2,1,0:T(2,128)}, u32[]{:S(2)}) copy-start(f32[3,1,1,2,256]{4,3,2,1,0:T(2,128)} %speed_ref.1) | copy-start | bytes 18436
  21.9 3.7 %collective-permute-start.5 = (f32[2,4,256]{2,1,0:T(4,128)S(1)}, f32[2,4,256]{2,1,0:T(4,128)S(1)}, u32[]{:S(2)}, u32[]{:S(2)}) collective-permute-start(f32[2,4,256]{2,1,0:T(4,128)S(1)} %get-tuple-element.11.refs_0_.own_ref), channel_id=1, source_target_pairs={{0,4},{4,0},{1,5},{5,1},{2,6},{6,2},{3,7},{7,3},{8,12},{12,8},{9,1... | collective-permute-start | bytes 24584 | tf_op jit(solution)/shard_map/ppermute | solution.py:258
  25.7 3.3 %collective-permute-start.6 = (f32[2,2,4,256]{3,2,1,0:T(4,128)S(1)}, f32[2,2,4,256]{3,2,1,0:T(4,128)S(1)}, u32[]{:S(2)}, u32[]{:S(2)}) collective-permute-start(f32[2,2,4,256]{3,2,1,0:T(4,128)S(1)} %get-tuple-element.19), channel_id=1, source_target_pairs={{0,8},{8,0},{16,24},{24,16},{1,9},{9,1},{17,25},{25,17},{2,10},{10... | collective-permute-start | bytes 49160 | tf_op jit(solution)/shard_map/ppermute | solution.py:262
  25.7 3.2 %collective-permute-start.7 = (f32[2,2,4,256]{3,2,1,0:T(4,128)S(1)}, f32[2,2,4,256]{3,2,1,0:T(4,128)S(1)}, u32[]{:S(2)}, u32[]{:S(2)}) collective-permute-start(f32[2,2,4,256]{3,2,1,0:T(4,128)S(1)} %get-tuple-element.19), channel_id=1, source_target_pairs={{0,24},{8,16},{16,8},{24,0},{1,25},{9,17},{17,9},{25,1},{2,26},{10... | collective-permute-start | bytes 49160 | tf_op jit(solution)/shard_map/ppermute | solution.py:261
  29.0 5.7 %collective-permute-start.8 = (f32[3,2,4,256]{3,2,1,0:T(4,128)S(1)}, f32[3,2,4,256]{3,2,1,0:T(4,128)S(1)}, u32[]{:S(2)}, u32[]{:S(2)}) collective-permute-start(f32[3,2,4,256]{3,2,1,0:T(4,128)S(1)} %get-tuple-element.15), channel_id=1, source_target_pairs={{0,1},{1,0},{2,3},{3,2},{4,5},{5,4},{6,7},{7,6},{8,9},{9,8},{10,11... | collective-permute-start | bytes 73736 | tf_op jit(solution)/shard_map/ppermute | solution.py:272
  29.7 5.6 %collective-permute-start.9 = (f32[3,2,4,256]{3,2,1,0:T(4,128)S(1)}, f32[3,2,4,256]{3,2,1,0:T(4,128)S(1)}, u32[]{:S(2)}, u32[]{:S(2)}) collective-permute-start(f32[3,2,4,256]{3,2,1,0:T(4,128)S(1)} %get-tuple-element.14), channel_id=1, source_target_pairs={{0,3},{1,2},{2,1},{3,0},{4,7},{5,6},{6,5},{7,4},{8,11},{9,10},{10,... | collective-permute-start | bytes 73736 | tf_op jit(solution)/shard_map/ppermute | solution.py:271
